TPU v7x, 512 devices: a whole 4x8x8 slice. The times are simulated.
512 devices in a mesh: dp: 8 (over z_hi, core), seq: 64 (over z_lo, x, y).
Axes of the slice: x: 4, y: 8, z: 8 (z_hi: 4, z_lo: 2; z = z_hi * 2 + z_lo), core: 2. Of those that a mesh axis runs over, the one named last changes fastest.
Arguments:
- query: bfloat16 [8, 8192, 2048], P('dp', 'seq'), may hold values from -32 to 32
- key: bfloat16 [8, 8192, 2048], P('dp', 'seq'), may hold values from -32 to 32
- value: bfloat16 [8, 8192, 2048], P('dp', 'seq'), may hold values from -12 to 12
- gains: float32 [4, 128], replicated, may hold values from 1 to 5.5
- d_mixed: bfloat16 [8, 2, 128, 32, 2048], P('dp', None, 'seq'), may hold values from -12 to 12
Outputs:
- mixed: bfloat16 [8, 2, 128, 32, 2048], P('dp', None, 'seq')
- query_grad: bfloat16 [8, 8192, 2048], P('dp', 'seq')
- key_grad: bfloat16 [8, 8192, 2048], P('dp', 'seq')
- value_grad: bfloat16 [8, 8192, 2048], P('dp', 'seq')
- gain_grads: float32 [4, 128], replicated
All inputs are finite; a program needn't handle non-finite values.
Results may differ from a plain program's by a relative error of at most 0.009.
The roundings to bfloat16 on the way count: a program that leaves them out, or rounds other values in their place, can miss the bound.
Values may be sent and summed in bfloat16 or wider, within the bound.
A program may use at most 64 MiB of HBM per device.

v0:
```python
import jax
import jax.numpy as jnp
from jax import lax
from jax.experimental import pallas as pl
from jax.experimental.pallas import tpu as pltpu
from jax.sharding import PartitionSpec as P

SEQ = 64
DP = 8
WIDTH = 2048
HALF = 1024
PART = 512
HD = 128
ROWS = 128
FRAMES = 32
EPS = 1e-06
SCALE = HD**-0.5
SCALE2 = SCALE * 1.4426950408889634
BF = jnp.bfloat16
F32 = jnp.float32


def dot(a, b, dims):
    return lax.dot_general(a, b, (dims, ((), ())), preferred_element_type=F32)


NN = ((1,), (0,))
NT = ((1,), (1,))
TN = ((0,), (0,))


def selector(column_of_row):
    row = lax.broadcasted_iota(jnp.int32, (256, 256), 0)
    column = lax.broadcasted_iota(jnp.int32, (256, 256), 1)
    return jnp.where(column == column_of_row(row), 1.0, 0.0).astype(BF)


def space_to_chunk(o):
    return (o & 3) * 64 + ((o >> 2) & 1) * 32 + (o >> 4) * 2 + ((o >> 3) & 1)


def chunk_to_space(i):
    return ((i & 31) >> 1) * 16 + (i & 1) * 8 + ((i >> 5) & 1) * 4 + (i >> 6)


def chunk_to_time(o):
    return (o & 15) * 16 + ((o >> 4) & 1) * 8 + ((o >> 5) & 1) * 4 + (o >> 6)


def time_to_chunk(i):
    return (i & 3) * 64 + (((i >> 2) & 1) * 2 + ((i >> 3) & 1)) * 16 + (i >> 4)


def hat(values):
    factor = lax.rsqrt(jnp.sum(values * values, axis=-1, keepdims=True) * (1.0 / HD) + EPS)
    return values * factor, factor


def softmax(scores):
    peak = jnp.max(scores, axis=-1, keepdims=True)
    raised = jnp.exp2((scores - peak) * SCALE2)
    return raised * (1.0 / jnp.sum(raised, axis=-1, keepdims=True))


def norm_back(x_hat, factor, gain, incoming):
    product = incoming * x_hat
    mean = jnp.sum(product * gain, axis=-1, keepdims=True) * (1.0 / HD)
    return factor * (incoming * gain - x_hat * mean), product


def fold(product):
    return jnp.sum(product.reshape(-1, 8, HD), axis=0)


def kernel(
    query, key, value, gains, d_mixed,
    mixed, query_grad, key_grad, value_grad, gain_grads,
    select, frame, d_time, probs, o_space, send_qk, send_o, got_qk, got_o,
    time_in, time_out, time_mixed, send_d, send_dqk, got_d, got_dqk, d_space, back, final,
    sums, gathered,
    own_sem, trade_send, trade_recv, mixed_in_sem, mixed_sem,
    qk_send, qk_recv, o_send, o_recv, d_send, d_recv, dqk_send, dqk_recv,
    out_sem, out_send, out_recv, sum_send, sum_recv,
):
    me = lax.axis_index("seq")
    sample = lax.axis_index("dp")
    z, x, y = me // 32, (me // 8) % 4, me % 8
    half, frame_at = me % 2, me // 2
    partner = me + 1 - 2 * half

    def peer(step):
        return (
            ((z + step // 32) % 2) * 32 + ((x + (step // 8) % 4) % 4) * 8 + (y + step % 8) % 8
        )

    def frame_peer(step):
        return (
            ((z + step // 16) % 2) * 16
            + ((x + (step // 4) % 4) % 4) * 4
            + (y // 2 + step % 4) % 4
        )

    inputs = (query, key, value)
    outputs = (query_grad, key_grad, value_grad)

    def own_copy(a, g):
        return pltpu.make_async_copy(
            inputs[a].at[:, pl.ds(half * HALF + g * PART, PART)],
            frame.at[a, half, :, pl.ds(g * PART, PART)],
            own_sem.at[a, g],
        )

    def trade_copy(a, g):
        return pltpu.make_async_remote_copy(
            src_ref=inputs[a].at[:, pl.ds((1 - half) * HALF + g * PART, PART)],
            dst_ref=frame.at[a, half, :, pl.ds(g * PART, PART)],
            send_sem=trade_send.at[a, g],
            recv_sem=trade_recv.at[a, g],
            device_id={"seq": partner},
            device_id_type=pl.DeviceIdType.MESH,
        )

    for g in range(2):
        for a in range(3):
            own_copy(a, g).start()
    mixed_in = pltpu.make_async_copy(d_mixed, d_time, mixed_in_sem)
    mixed_in.start()

    barrier = pltpu.get_barrier_semaphore()

    @pl.loop(1, SEQ)
    def _(step):
        pl.semaphore_signal(
            barrier, inc=1, device_id={"seq": peer(step)}, device_id_type=pl.DeviceIdType.MESH
        )

    @pl.loop(1, DP)
    def _(step):
        pl.semaphore_signal(
            barrier,
            inc=1,
            device_id={"dp": (sample + step) % DP},
            device_id_type=pl.DeviceIdType.MESH,
        )

    for i, source in enumerate((space_to_chunk, chunk_to_space, chunk_to_time, time_to_chunk)):
        select[i] = selector(source)
    sums[...] = jnp.zeros_like(sums)

    pl.semaphore_wait(barrier, SEQ - 1 + DP - 1)

    for g in range(2):
        for a in range(3):
            trade_copy(a, g).start()

    gain = [gains[i : i + 1, :] for i in range(4)]

    def send_all(source, target, send_sem, recv_sem):
        pltpu.make_async_copy(source.at[me], target.at[frame_at], recv_sem).start()

        @pl.loop(1, SEQ)
        def _(step):
            to = peer(step)
            pltpu.make_async_remote_copy(
                src_ref=source.at[to],
                dst_ref=target.at[frame_at],
                send_sem=send_sem,
                recv_sem=recv_sem,
                device_id={"seq": to},
                device_id_type=pl.DeviceIdType.MESH,
            ).start()

    def wait_bytes(ref, sem):
        pltpu.make_async_copy(ref, ref, sem).wait()

    @pl.loop(0, 2)
    def _(g):
        for a in range(2):
            own_copy(a, g).wait()
            trade_copy(a, g).wait_recv()

        @pl.loop(0, 4)
        def _(b):
            pieces = []
            for a in range(2):
                pieces.append(
                    jnp.concatenate(
                        [
                            frame[a, r, pl.ds(b * 32, 32), pl.ds(g * PART + h * HD, HD)]
                            for h in range(4)
                            for r in range(2)
                        ],
                        axis=0,
                    )
                )
            moved = dot(select[0], jnp.concatenate(pieces, axis=1), NN).astype(BF)
            for a in range(2):
                send_qk[g, pl.ds(b * 16, 16), a] = moved[:, a * HD : (a + 1) * HD].reshape(16, 16, HD)

        slot = g * 2 + half
        send_all(send_qk.at[g], got_qk.at[slot], qk_send.at[g], qk_recv.at[slot])
        own_copy(2, g).wait()
        trade_copy(2, g).wait_recv()

        @pl.loop(0, 4)
        def _(h):
            columns = pl.ds(pl.multiple_of(g * PART + h * HD, HD), HD)
            q_hat, _ = hat(frame[0, :, :, columns].reshape(256, HD).astype(F32))
            k_hat, _ = hat(frame[1, :, :, columns].reshape(256, HD).astype(F32))
            q = (q_hat * gain[0]).astype(BF)
            k = (k_hat * gain[1]).astype(BF)
            weights = softmax(dot(q, k, NT))
            probs[g * 4 + h] = weights
            result = dot(weights.astype(BF), frame[2, :, :, columns].reshape(256, HD), NN)
            o_space[g, h] = result.astype(BF).reshape(2, 4, 32, HD)

        @pl.loop(0, 4)
        def _(b):
            moved = dot(select[0], o_space[g, :, :, b].reshape(256, HD), NN).astype(BF)
            send_o[g, pl.ds(b * 16, 16)] = moved.reshape(16, 16, HD)

        send_all(send_o.at[g], got_o.at[slot], o_send.at[g], o_recv.at[slot])

    mixed_in.wait()
    group = lax.broadcasted_iota(jnp.int32, (ROWS, ROWS), 0) // FRAMES
    same = group == lax.broadcasted_iota(jnp.int32, (ROWS, ROWS), 1) // FRAMES

    @pl.loop(0, 4)
    def _(t):
        to_half = t % 2
        g = t // 2
        wait_bytes(got_qk.at[t], qk_recv.at[t])
        wait_bytes(got_o.at[t], o_recv.at[t])
        for part in range(2):
            here = pl.ds(part * 16, 16)
            blocks = [got_qk[t, here, 0], got_qk[t, here, 1], got_o[t, here]]
            moved = dot(
                select[2], jnp.concatenate([b.reshape(256, HD) for b in blocks], axis=1), NN
            )
            for a in range(3):
                time_in[a, :, :, part] = moved[:, a * HD : (a + 1) * HD].reshape(4, 4, 16, HD)

        @pl.loop(0, 4)
        def _(h):
            columns = pl.ds(pl.multiple_of(to_half * HALF + g * PART + h * HD, HD), HD)
            q_hat, q_factor = hat(time_in[0, h].reshape(ROWS, HD))
            k_hat, k_factor = hat(time_in[1, h].reshape(ROWS, HD))
            o = time_in[2, h].reshape(ROWS, HD).astype(BF)
            q = (q_hat * gain[2]).astype(BF)
            k = (k_hat * gain[3]).astype(BF)
            weights = softmax(jnp.where(same, dot(q, k, NT), -1e30))
            rounded = weights.astype(BF)
            result = dot(rounded, o, NN).astype(BF)
            time_mixed[:, columns] = result
            d_out = d_time[:, columns]
            delta = jnp.sum(d_out.astype(F32) * result.astype(F32), axis=-1, keepdims=True)
            d_scores = (weights * (dot(d_out, o, NT) - delta) * SCALE).astype(BF)
            d_q, product = norm_back(q_hat, q_factor, gain[2], dot(d_scores, k, NN))
            sums[2] += fold(product)
            d_k, product = norm_back(k_hat, k_factor, gain[3], dot(d_scores, q, TN))
            sums[3] += fold(product)
            d_o = dot(rounded, d_out, TN)
            for a, one in enumerate((d_o, d_q, d_k)):
                time_out[a, h] = one.astype(BF).reshape(4, 2, 16, HD)

        for part in range(2):
            moved = dot(
                select[3],
                jnp.concatenate([time_out[a, :, :, part].reshape(256, HD) for a in range(3)], axis=1),
                NN,
            ).astype(BF)
            here = pl.ds(part * 16, 16)
            send_d[t, here] = moved[:, :HD].reshape(16, 16, HD)
            send_dqk[t, here, 0] = moved[:, HD : 2 * HD].reshape(16, 16, HD)
            send_dqk[t, here, 1] = moved[:, 2 * HD :].reshape(16, 16, HD)

        def send_back(source, target, send_sem, recv_sem):
            def one(step):
                to = frame_peer(step)
                pltpu.make_async_remote_copy(
                    src_ref=source.at[to],
                    dst_ref=target.at[me],
                    send_sem=send_sem,
                    recv_sem=recv_sem,
                    device_id={"seq": to * 2 + to_half},
                    device_id_type=pl.DeviceIdType.MESH,
                ).start()

            @pl.when(to_half == half)
            def _():
                pltpu.make_async_copy(source.at[frame_at], target.at[me], recv_sem).start()

            @pl.when(to_half != half)
            def _():
                one(0)

            pl.loop(1, FRAMES)(one)

        send_back(send_d.at[t], got_d.at[g], d_send, d_recv.at[g])
        send_back(send_dqk.at[t], got_dqk.at[g], dqk_send, dqk_recv.at[g])

    mixed_out = pltpu.make_async_copy(time_mixed, mixed, mixed_sem)
    mixed_out.start()

    def out_own(a, g):
        return pltpu.make_async_copy(
            final.at[a, half, :, pl.ds(g * PART, PART)],
            outputs[a].at[:, pl.ds(half * HALF + g * PART, PART)],
            out_sem.at[a, g],
        )

    def out_trade(a, g):
        return pltpu.make_async_remote_copy(
            src_ref=final.at[a, 1 - half, :, pl.ds(g * PART, PART)],
            dst_ref=outputs[a].at[:, pl.ds(half * HALF + g * PART, PART)],
            send_sem=out_send.at[a, g],
            recv_sem=out_recv.at[a, g],
            device_id={"seq": partner},
            device_id_type=pl.DeviceIdType.MESH,
        )

    @pl.loop(0, 2)
    def _(g):
        wait_bytes(got_d.at[g], d_recv.at[g])

        @pl.loop(0, 4)
        def _(b):
            moved = dot(select[1], got_d[g, pl.ds(b * 16, 16)].reshape(256, HD), NN).astype(BF)
            d_space[:, :, b] = moved.reshape(4, 2, 32, HD)

        @pl.loop(0, 4)
        def _(h):
            columns = pl.ds(pl.multiple_of(g * PART + h * HD, HD), HD)
            q_hat, q_factor = hat(frame[0, :, :, columns].reshape(256, HD).astype(F32))
            k_hat, k_factor = hat(frame[1, :, :, columns].reshape(256, HD).astype(F32))
            q = (q_hat * gain[0]).astype(BF)
            k = (k_hat * gain[1]).astype(BF)
            v = frame[2, :, :, columns].reshape(256, HD)
            weights = probs[g * 4 + h]
            d_out = d_space[h].reshape(256, HD)
            result = o_space[g, h].reshape(256, HD)
            delta = jnp.sum(d_out.astype(F32) * result.astype(F32), axis=-1, keepdims=True)
            d_scores = (weights * (dot(d_out, v, NT) - delta) * SCALE).astype(BF)
            d_q, product = norm_back(q_hat, q_factor, gain[0], dot(d_scores, k, NN))
            sums[0] += fold(product)
            back[0, h] = d_q.reshape(2, 4, 32, HD)
            d_k, product = norm_back(k_hat, k_factor, gain[1], dot(d_scores, q, TN))
            sums[1] += fold(product)
            back[1, h] = d_k.reshape(2, 4, 32, HD)
            d_v = dot(weights.astype(BF), d_out, TN)
            final[2, :, :, columns] = d_v.astype(BF).reshape(2, ROWS, HD)

        wait_bytes(got_dqk.at[g], dqk_recv.at[g])

        @pl.loop(0, 4)
        def _(b):
            here = pl.ds(b * 16, 16)
            moved = dot(
                select[1],
                jnp.concatenate([got_dqk[g, here, a].reshape(256, HD) for a in range(2)], axis=1),
                NN,
            )
            for a in range(2):
                for h in range(4):
                    for r in range(2):
                        at = h * 64 + r * 32
                        total = moved[at : at + 32, a * HD : (a + 1) * HD] + back[a, h, r, b]
                        columns = pl.ds(pl.multiple_of(g * PART + h * HD, HD), HD)
                        final[a, r, pl.ds(b * 32, 32), columns] = total.astype(BF)

        for a in range(3):
            out_trade(a, g).start()
            out_own(a, g).start()

    own = jnp.sum(sums[...], axis=1)
    total = jnp.concatenate([own, jnp.zeros_like(own)], axis=0)
    rounds = (
        (z * 4 + x, lambda at: {"seq": at * 8 + y}),
        (y, lambda at: {"seq": z * 32 + x * 8 + at}),
        (sample, lambda at: {"dp": at}),
    )
    for i, (place, device) in enumerate(rounds):
        gathered[i, place] = total

        @pl.loop(1, 8)
        def _(step):
            pltpu.make_async_remote_copy(
                src_ref=gathered.at[i, place],
                dst_ref=gathered.at[i, place],
                send_sem=sum_send.at[i],
                recv_sem=sum_recv.at[i],
                device_id=device((place + step) % 8),
                device_id_type=pl.DeviceIdType.MESH,
            ).start()

        wait_bytes(gathered.at[i, pl.ds(0, 7)], sum_recv.at[i])
        total = jnp.sum(gathered[i], axis=0)
    gain_grads[...] = total[0:4]

    for i in range(3):
        wait_bytes(gathered.at[i, pl.ds(0, 7)], sum_send.at[i])
    for g in range(2):
        for a in range(3):
            trade_copy(a, g).wait_send()
            out_trade(a, g).wait()
            out_own(a, g).wait()
        wait_bytes(send_qk.at[g, pl.ds(0, SEQ - 1)], qk_send.at[g])
        wait_bytes(send_o.at[g, pl.ds(0, SEQ - 1)], o_send.at[g])
    wait_bytes(got_d.at[:, pl.ds(0, SEQ - 1)], d_send)
    wait_bytes(got_dqk.at[:, pl.ds(0, SEQ - 1)], dqk_send)
    mixed_out.wait()


def body(query, key, value, gains, d_mixed):
    wide = (ROWS, WIDTH)
    any_spec = pl.BlockSpec(memory_space=pl.ANY)
    vmem_spec = pl.BlockSpec(memory_space=pltpu.VMEM)
    dma = pltpu.SemaphoreType.DMA
    mixed, query_grad, key_grad, value_grad, gain_grads = pl.pallas_call(
        kernel,
        out_shape=[jax.ShapeDtypeStruct(wide, BF)] * 4 + [jax.ShapeDtypeStruct((4, HD), F32)],
        in_specs=[any_spec, any_spec, any_spec, vmem_spec, any_spec],
        out_specs=[any_spec, any_spec, any_spec, any_spec, vmem_spec],
        scratch_shapes=[
            pltpu.VMEM((4, 256, 256), BF),
            pltpu.VMEM((3, 2, ROWS, HALF), BF),
            pltpu.VMEM(wide, BF),
            pltpu.VMEM((8, 256, 256), F32),
            pltpu.VMEM((2, 4, 2, 4, 32, HD), BF),
            pltpu.VMEM((2, SEQ, 2, 16, HD), BF),
            pltpu.VMEM((2, SEQ, 16, HD), BF),
            pltpu.VMEM((4, FRAMES, 2, 16, HD), BF),
            pltpu.VMEM((4, FRAMES, 16, HD), BF),
            pltpu.VMEM((3, 4, 4, 2, 16, HD), F32),
            pltpu.VMEM((3, 4, 4, 2, 16, HD), BF),
            pltpu.VMEM(wide, BF),
            pltpu.VMEM((4, FRAMES, 16, HD), BF),
            pltpu.VMEM((4, FRAMES, 2, 16, HD), BF),
            pltpu.VMEM((2, SEQ, 16, HD), BF),
            pltpu.VMEM((2, SEQ, 2, 16, HD), BF),
            pltpu.VMEM((4, 2, 4, 32, HD), BF),
            pltpu.VMEM((2, 4, 2, 4, 32, HD), F32),
            pltpu.VMEM((3, 2, ROWS, HALF), BF),
            pltpu.VMEM((4, 8, HD), F32),
            pltpu.VMEM((3, 8, 8, HD), F32),
            dma((3, 2)),
            dma((3, 2)),
            dma((3, 2)),
            dma,
            dma,
            dma((2,)),
            dma((4,)),
            dma((2,)),
            dma((4,)),
            dma,
            dma((2,)),
            dma,
            dma((2,)),
            dma((3, 2)),
            dma((3, 2)),
            dma((3, 2)),
            dma((3,)),
            dma((3,)),
        ],
        compiler_params=pltpu.CompilerParams(
            collective_id=0, has_side_effects=True, vmem_limit_bytes=40 * 2**20
        ),
        cost_estimate=pl.CostEstimate(flops=2 * 10**9, bytes_accessed=2**22, transcendentals=10**6),
        name="space_time_attention",
    )(query.reshape(wide), key.reshape(wide), value.reshape(wide), gains, d_mixed.reshape(wide))
    return (
        mixed.reshape(d_mixed.shape),
        query_grad.reshape(query.shape),
        key_grad.reshape(key.shape),
        value_grad.reshape(value.shape),
        gain_grads,
    )


def solution(mesh):
    placed = (
        P("dp", "seq", None),
        P("dp", "seq", None),
        P("dp", "seq", None),
        P(),
        P("dp", None, "seq", None, None),
    )
    return jax.shard_map(
        body,
        mesh=mesh,
        in_specs=placed,
        out_specs=(
            P("dp", None, "seq", None, None),
            P("dp", "seq", None),
            P("dp", "seq", None),
            P("dp", "seq", None),
            P(),
        ),
        check_vma=False,
    )
```

profile of v0, /device:TPU:1, one launch (start us, length us, event | category | flops | bytes accessed | tf_op | source)
XLA Modules:
  0.0 136.4 jit_solution(13297493362757550845)
XLA Ops:
  0.6 0.0 copy-start.4
  0.6 0.7 copy-done.4
  1.3 0.0 copy-start
  1.3 1.0 copy-done
  2.4 0.0 copy-start.1
  2.4 1.0 copy-done.1
  3.4 0.0 copy-start.2
  3.4 1.0 copy-done.2
  4.4 0.0 copy-start.3
  4.4 1.0 copy-done.3
  5.5 127.2 %space_time_attention.1 = (bf16[128,2048]{1,0:T(8,128)(2,1)S(1)}, bf16[128,2048]{1,0:T(8,128)(2,1)S(1)}, bf16[128,2048]{1,0:T(8,128)(2,1)S(1)}, bf16[128,2048]{1,0:T(8,128)(2,1)S(1)}, f32[4,128]{1,0:T(4,128)S(1)}) custom-call(bf16[128,2048]{1,0:T(8,128)(2,1)S(1)} %bitcast.12, bf16[128,2048]{1,0:T(8,128)(2,1)S(1)} %bitcast.13, ...), custom_call_target="tpu_custom_call" | custom-call | flops 2000000000 | bytes 4194304 | tf_op jit(solution)/shard_map/space_time_attention/pallas_call | solution.py:419
  132.7 0.8 copy.15
  133.5 0.8 copy.16
  134.3 0.8 copy.17
  135.1 0.8 copy.18
  135.8 0.6 copy.19
Async XLA Ops:
  0.6 0.7 copy-start.4
  1.3 1.0 copy-start
  2.4 1.0 copy-start.1
  3.4 1.0 copy-start.2
  4.4 1.0 copy-start.3
where the time goes:
time: 137 us; the launch traced here: 136 us
  Pallas kernels  127 us (93%)
  local copies, waits for them, and re-layouts  8.59 us (6%)
    pallas_call x1, Pallas kernels, body(): pl.pallas_call(kernel, out_shape=[jax.ShapeDtypeStruct(wide, BF)] * 4 + [...  127 us
    unnamed x15, local copies, waits for them, and re-layouts  8.59 us

commit v1 on v0

v1 whole, which is shorter than its diff:
```python
import jax
import jax.numpy as jnp
from jax import lax
from jax.experimental import pallas as pl
from jax.experimental.pallas import tpu as pltpu
from jax.sharding import PartitionSpec as P

SEQ = 64
DP = 8
WIDTH = 2048
HALF = 1024
PART = 512
HD = 128
ROWS = 128
FRAMES = 32
EPS = 1e-06
SCALE = HD**-0.5
SCALE2 = SCALE * 1.4426950408889634
BF = jnp.bfloat16
F32 = jnp.float32


def dot(a, b, dims):
    return lax.dot_general(a, b, (dims, ((), ())), preferred_element_type=F32)


NN = ((1,), (0,))
NT = ((1,), (1,))
TN = ((0,), (0,))


def selector(column_of_row):
    row = lax.broadcasted_iota(jnp.int32, (256, 256), 0)
    column = lax.broadcasted_iota(jnp.int32, (256, 256), 1)
    return jnp.where(column == column_of_row(row), 1.0, 0.0).astype(BF)


def from_space(o):
    return (o & 3) * 64 + ((o >> 2) & 1) * 32 + (o >> 4) * 2 + ((o >> 3) & 1)


def to_space(i):
    return ((i & 31) >> 1) * 16 + (i & 1) * 8 + ((i >> 5) & 1) * 4 + (i >> 6)


def to_time(o):
    return (o & 15) * 16 + ((o >> 4) & 1) * 8 + ((o >> 5) & 1) * 4 + (o >> 6)


def from_time(i):
    return (i & 3) * 64 + (((i >> 2) & 1) * 2 + ((i >> 3) & 1)) * 16 + (i >> 4)


def from_rows(o):
    return (o & 7) * 32 + (o >> 4) * 2 + ((o >> 3) & 1)


def to_rows(i):
    return ((i & 31) >> 1) * 16 + (i & 1) * 8 + (i >> 5)


def to_time8(o):
    return (o & 7) * 32 + ((o >> 4) & 1) * 16 + ((o >> 3) & 1) * 8 + (o >> 5)


def from_time8(c):
    return (c & 7) * 32 + (((c >> 4) & 1) * 2 + ((c >> 3) & 1)) * 8 + (c >> 5)


SELECTORS = (from_space, to_space, to_time, from_time, from_rows, to_rows, to_time8, from_time8)


def hat(values):
    factor = lax.rsqrt(jnp.sum(values * values, axis=-1, keepdims=True) * (1.0 / HD) + EPS)
    return values * factor, factor


def softmax(scores):
    peak = jnp.max(scores, axis=-1, keepdims=True)
    raised = jnp.exp2((scores - peak) * SCALE2)
    return raised * (1.0 / jnp.sum(raised, axis=-1, keepdims=True))


def norm_back(x_hat, factor, gain, incoming):
    product = incoming * x_hat
    mean = jnp.sum(product * gain, axis=-1, keepdims=True) * (1.0 / HD)
    return factor * (incoming * gain - x_hat * mean), product


def fold(product):
    return jnp.sum(product.reshape(-1, 8, HD), axis=0)


def kernel(
    query, key, value, gains_in, d_mixed,
    mixed, query_grad, key_grad, value_grad, gain_grads,
    gains, select, native, frame, d_time, probs, o_space, send_native, send_relay, send_o, got_qk, got_o,
    time_qk, time_o, time_d, time_dqk, time_mixed, send_d, send_dqk, got_d, got_own, got_head,
    got_token, d_space, back, final_out, final_own, final_in, final_sum, sums, gathered,
    gains_sem, native_sem, own_sem, trade_send, trade_recv, mixed_in_sem, mixed_sem,
    native_send, relay_send, qk_recv, o_send, o_recv, d_send, d_recv,
    head_send, token_send, back_send, head_recv, token_recv, back_recv,
    out_sem, out_send, out_recv, sum_sem, sum_send, sum_recv,
):
    me = lax.axis_index("seq")
    sample = lax.axis_index("dp")
    z, x, y = me // 32, (me // 8) % 4, me % 8
    half, frame_at = me % 2, me // 2
    other = 1 - half
    partner = me + 1 - 2 * half

    def device_at(step, dy):
        return ((z + step // 16) % 2) * 32 + ((x + (step // 4) % 4) % 4) * 8 + (y + 8 + dy) % 8

    def peer(step):
        return (
            ((z + step // 32) % 2) * 32 + ((x + (step // 8) % 4) % 4) * 8 + (y + step % 8) % 8
        )

    def near_peer(step):
        return device_at(step, (step % 4) * (2 * half - 1))

    def far_peer(step):
        return device_at(step, (step % 4 + 1) * (1 - 2 * half))

    def frame_peer(step):
        return (
            ((z + step // 16) % 2) * 16
            + ((x + (step // 4) % 4) % 4) * 4
            + (y // 2 + step % 4) % 4
        )

    def remote(source, target, send_sem, recv_sem, to):
        return pltpu.make_async_remote_copy(
            src_ref=source,
            dst_ref=target,
            send_sem=send_sem,
            recv_sem=recv_sem,
            device_id=to if isinstance(to, dict) else {"seq": to},
            device_id_type=pl.DeviceIdType.MESH,
        )

    def wait_bytes(ref, sem):
        pltpu.make_async_copy(ref, ref, sem).wait()

    inputs = (query, key, value)
    outputs = (query_grad, key_grad, value_grad)

    def own_copy(a, g):
        return pltpu.make_async_copy(
            inputs[a].at[:, pl.ds(half * HALF + g * PART, PART)],
            frame.at[a, half, :, pl.ds(g * PART, PART)],
            own_sem.at[a, g],
        )

    def trade_copy(a, g):
        return remote(
            inputs[a].at[:, pl.ds(other * HALF + g * PART, PART)],
            frame.at[a, half, :, pl.ds(g * PART, PART)],
            trade_send.at[a, g],
            trade_recv.at[a, g],
            partner,
        )

    gains_copy = pltpu.make_async_copy(gains_in, gains, gains_sem)
    gains_copy.start()
    native_copies = [
        pltpu.make_async_copy(inputs[a], native.at[a], native_sem.at[a]) for a in range(2)
    ]
    for copy in native_copies:
        copy.start()
    for g in range(2):
        for a in range(3):
            own_copy(a, g).start()
    mixed_in = pltpu.make_async_copy(d_mixed, d_time, mixed_in_sem)
    mixed_in.start()
    got_head[...] = jnp.zeros_like(got_head)
    got_token[...] = jnp.zeros_like(got_token)

    barrier = pltpu.get_barrier_semaphore()

    @pl.loop(1, SEQ)
    def _(step):
        pl.semaphore_signal(
            barrier, inc=1, device_id={"seq": peer(step)}, device_id_type=pl.DeviceIdType.MESH
        )

    @pl.loop(1, DP)
    def _(step):
        pl.semaphore_signal(
            barrier,
            inc=1,
            device_id={"dp": (sample + step) % DP},
            device_id_type=pl.DeviceIdType.MESH,
        )

    pl.semaphore_wait(barrier, SEQ - 1 + DP - 1)

    for g in range(2):
        for a in range(3):
            trade_copy(a, g).start()

    for i, source in enumerate(SELECTORS):
        select[i] = selector(source)
    sums[...] = jnp.zeros_like(sums)
    gains_copy.wait()
    gain = [gains[i : i + 1, :] for i in range(4)]

    def rows_to_units(source, block, first, target):
        pieces = [
            jnp.concatenate(
                [source(a)[pl.ds(block * 32, 32), pl.ds(first + h * HD, HD)] for h in range(8)], axis=0
            )
            for a in range(2)
        ]
        moved = dot(select[4], jnp.concatenate(pieces, axis=1), NN).astype(BF)
        for a in range(2):
            target(pl.ds(block * 16, 16), a, moved[:, a * HD : (a + 1) * HD].reshape(16, 16, HD))

    for copy in native_copies:
        copy.wait()

    for hh in range(2):

        def put(devices, a, units):
            send_native[devices, hh, a] = units

        for block in range(4):
            rows_to_units(lambda a: native.at[a], block, hh * HALF, put)

    @pl.loop(0, 2)
    def _(g):
        for a in range(3):
            own_copy(a, g).wait()
            trade_copy(a, g).wait_recv()

        @pl.when(g == 0)
        def _():
            pltpu.make_async_copy(send_native.at[me], got_qk.at[frame_at, half], qk_recv).start()

            @pl.loop(1, 32)
            def _(step):
                to = near_peer(step)
                remote(send_native.at[to], got_qk.at[frame_at, half], native_send, qk_recv, to).start()

            @pl.loop(0, 32)
            def _(step):
                to = far_peer(step)
                remote(
                    send_native.at[to, half], got_qk.at[frame_at, half, half], native_send, qk_recv, to
                ).start()

        @pl.loop(0, 4)
        def _(h):
            columns = pl.ds(pl.multiple_of(g * PART + h * HD, HD), HD)
            q_hat, _ = hat(frame[0, :, :, columns].reshape(256, HD).astype(F32))
            k_hat, _ = hat(frame[1, :, :, columns].reshape(256, HD).astype(F32))
            q = (q_hat * gain[0]).astype(BF)
            k = (k_hat * gain[1]).astype(BF)
            weights = softmax(dot(q, k, NT))
            probs[g * 4 + h] = weights
            result = dot(weights.astype(BF), frame[2, :, :, columns].reshape(256, HD), NN)
            o_space[g, h] = result.astype(BF).reshape(2, 4, 32, HD)

        for b in range(4):
            moved = dot(select[0], o_space[g, :, :, b].reshape(256, HD), NN).astype(BF)
            send_o[g, pl.ds(b * 16, 16)] = moved.reshape(16, 16, HD)

        slot = g * 2 + half
        pltpu.make_async_copy(send_o.at[g, me], got_o.at[slot, frame_at], o_recv.at[slot]).start()

        @pl.loop(1, SEQ)
        def _(step):
            to = peer(step)
            remote(
                send_o.at[g, to], got_o.at[slot, frame_at], o_send.at[g], o_recv.at[slot], to
            ).start()

    def put_relay(devices, a, units):
        send_relay[devices, a] = units

    for block in range(4):
        rows_to_units(lambda a: frame.at[a, other], block, 0, put_relay)

    pltpu.make_async_copy(send_relay.at[me], got_qk.at[frame_at, other, half], qk_recv).start()

    @pl.loop(1, 32)
    def _(step):
        to = near_peer(step)
        remote(
            send_relay.at[to], got_qk.at[frame_at, other, half], relay_send, qk_recv, to
        ).start()

    wait_bytes(got_qk, qk_recv)
    for hh in range(2):
        for part in range(4):
            here = pl.ds(part * 8, 8)
            units = [got_qk[here, :, hh, a].reshape(256, HD) for a in range(2)]
            moved = dot(select[6], jnp.concatenate(units, axis=1), NN)
            for a in range(2):
                time_qk[hh, a, :, :, part] = moved[:, a * HD : (a + 1) * HD].reshape(8, 4, 8, HD)

    mixed_in.wait()
    group = lax.broadcasted_iota(jnp.int32, (ROWS, ROWS), 0) // FRAMES
    same = group == lax.broadcasted_iota(jnp.int32, (ROWS, ROWS), 1) // FRAMES

    @pl.loop(0, 4)
    def _(t):
        hh = t % 2
        g = t // 2
        wait_bytes(got_o.at[t], o_recv.at[t])
        for part in range(2):
            units = got_o[t, pl.ds(part * 16, 16)].reshape(256, HD)
            time_o[:, :, part] = dot(select[2], units, NN).astype(BF).reshape(4, 4, 16, HD)

        heads = range(4)

        def each(one, *stacked):
            return jnp.concatenate(
                [one(*(values[h * ROWS : (h + 1) * ROWS] for values in stacked)) for h in heads], axis=0
            )

        columns = [
            pl.ds(pl.multiple_of(hh * HALF + g * PART + h * HD, HD), HD) for h in heads
        ]
        q_hat, q_factor = hat(time_qk[hh, 0, pl.ds(g * 4, 4)].reshape(4 * ROWS, HD))
        k_hat, k_factor = hat(time_qk[hh, 1, pl.ds(g * 4, 4)].reshape(4 * ROWS, HD))
        o = time_o[...].reshape(4 * ROWS, HD)
        q = (q_hat * gain[2]).astype(BF)
        k = (k_hat * gain[3]).astype(BF)
        scores = each(lambda q, k: jnp.where(same, dot(q, k, NT), -1e30), q, k)
        weights = softmax(scores)
        rounded = weights.astype(BF)
        result = each(lambda w, o: dot(w, o, NN), rounded, o).astype(BF)
        for h in heads:
            time_mixed[:, columns[h]] = result[h * ROWS : (h + 1) * ROWS]
        d_out = jnp.concatenate([d_time[:, columns[h]] for h in heads], axis=0)
        delta = jnp.sum(d_out.astype(F32) * result.astype(F32), axis=-1, keepdims=True)
        d_weights = each(lambda d, o: dot(d, o, NT), d_out, o)
        d_scores = (weights * (d_weights - delta) * SCALE).astype(BF)
        time_d[...] = (
            each(lambda w, d: dot(w, d, TN), rounded, d_out).astype(BF).reshape(4, 4, 2, 16, HD)
        )
        d_q, product = norm_back(
            q_hat, q_factor, gain[2], each(lambda s, k: dot(s, k, NN), d_scores, k)
        )
        sums[2] += fold(product)
        time_dqk[hh, 0, pl.ds(g * 4, 4)] = d_q.reshape(4, 4, 4, 8, HD)
        d_k, product = norm_back(
            k_hat, k_factor, gain[3], each(lambda s, q: dot(s, q, TN), d_scores, q)
        )
        sums[3] += fold(product)
        time_dqk[hh, 1, pl.ds(g * 4, 4)] = d_k.reshape(4, 4, 4, 8, HD)

        for part in range(2):
            moved = dot(select[3], time_d[:, :, part].reshape(256, HD), NN).astype(BF)
            send_d[t, pl.ds(part * 16, 16)] = moved.reshape(16, 16, HD)

        def send_one(step):
            to = frame_peer(step)
            remote(send_d.at[t, to], got_d.at[g, me], d_send, d_recv.at[g], to * 2 + hh).start()

        @pl.when(hh == half)
        def _():
            pltpu.make_async_copy(send_d.at[t, frame_at], got_d.at[g, me], d_recv.at[g]).start()

        @pl.when(hh != half)
        def _():
            send_one(0)

        pl.loop(1, FRAMES)(send_one)

    mixed_out = pltpu.make_async_copy(time_mixed, mixed, mixed_sem)
    mixed_out.start()

    for hh in range(2):
        for part in range(4):
            units = [time_dqk[hh, a, :, :, part].reshape(256, HD).astype(BF) for a in range(2)]
            moved = dot(select[7], jnp.concatenate(units, axis=1), NN).astype(BF)
            for a in range(2):
                send_dqk[hh, pl.ds(part * 8, 8), :, a] = moved[:, a * HD : (a + 1) * HD].reshape(
                    8, 2, 16, HD
                )

    def nearer(frame_to):
        return ((y + 11 - 2 * (frame_to % 4)) % 8) // 4

    pltpu.make_async_copy(send_dqk.at[half, frame_at, other], got_head.at[me], head_recv).start()

    @pl.loop(1, FRAMES)
    def _(step):
        to = frame_peer(step)
        side = nearer(to)
        remote(
            send_dqk.at[side, to, 1 - side], got_head.at[me], head_send, head_recv, to * 2 + side
        ).start()

    pltpu.make_async_copy(send_dqk.at[half, frame_at, half], got_own.at[me], back_recv).start()
    remote(
        send_dqk.at[other, frame_at, other], got_own.at[me], back_send, back_recv, partner
    ).start()
    pltpu.make_async_copy(send_dqk.at[other, frame_at, half], got_token.at[me], token_recv).start()

    @pl.loop(1, FRAMES)
    def _(step):
        to = frame_peer(step)
        side = nearer(to)
        remote(
            send_dqk.at[1 - side, to, side], got_token.at[me], token_send, token_recv, to * 2 + side
        ).start()
        for hh in range(2):
            remote(
                send_dqk.at[hh, to, hh], got_own.at[me], back_send, back_recv, to * 2 + hh
            ).start()

    def out_own(a, g):
        return pltpu.make_async_copy(
            final_own.at[a, :, pl.ds(g * PART, PART)],
            outputs[a].at[:, pl.ds(half * HALF + g * PART, PART)],
            out_sem.at[a, g],
        )

    def out_trade(a, g):
        place = half * HALF + g * PART
        target = value_grad.at[:, pl.ds(place, PART)] if a == 2 else final_in.at[a, :, pl.ds(g * PART, PART)]
        return remote(
            final_out.at[a, :, pl.ds(g * PART, PART)],
            target,
            out_send.at[a, g],
            out_recv.at[a, g],
            partner,
        )

    def units_to_rows(units, block):
        here = pl.ds(block * 16, 16)
        pieces = [units[here, a].reshape(256, HD) for a in range(2)]
        return dot(select[5], jnp.concatenate(pieces, axis=1), NN)

    @pl.loop(0, 2)
    def _(g):
        wait_bytes(got_d.at[g], d_recv.at[g])

        for b in range(4):
            moved = dot(select[1], got_d[g, pl.ds(b * 16, 16)].reshape(256, HD), NN).astype(BF)
            d_space[:, :, b] = moved.reshape(4, 2, 32, HD)

        @pl.loop(0, 4)
        def _(h):
            columns = pl.ds(pl.multiple_of(g * PART + h * HD, HD), HD)
            q_hat, q_factor = hat(frame[0, :, :, columns].reshape(256, HD).astype(F32))
            k_hat, k_factor = hat(frame[1, :, :, columns].reshape(256, HD).astype(F32))
            q = (q_hat * gain[0]).astype(BF)
            k = (k_hat * gain[1]).astype(BF)
            v = frame[2, :, :, columns].reshape(256, HD)
            weights = probs[g * 4 + h]
            d_out = d_space[h].reshape(256, HD)
            result = o_space[g, h].reshape(256, HD)
            delta = jnp.sum(d_out.astype(F32) * result.astype(F32), axis=-1, keepdims=True)
            d_scores = (weights * (dot(d_out, v, NT) - delta) * SCALE).astype(BF)
            d_q, product = norm_back(q_hat, q_factor, gain[0], dot(d_scores, k, NN))
            sums[0] += fold(product)
            back[0, g * 4 + h] = d_q.reshape(2, ROWS, HD)
            d_k, product = norm_back(k_hat, k_factor, gain[1], dot(d_scores, q, TN))
            sums[1] += fold(product)
            back[1, g * 4 + h] = d_k.reshape(2, ROWS, HD)
            d_v = dot(weights.astype(BF), d_out, TN).astype(BF).reshape(2, ROWS, HD)
            final_out[2, :, columns] = lax.select(half == 0, d_v[1], d_v[0])
            final_own[2, :, columns] = lax.select(half == 0, d_v[0], d_v[1])

        out_trade(2, g).start()
        out_own(2, g).start()

    def add_units(units, r, target):
        for block in range(4):
            moved = units_to_rows(units, block)
            here = pl.ds(block * 32, 32)
            for a in range(2):
                for h in range(8):
                    total = moved[h * 32 : h * 32 + 32, a * HD : (a + 1) * HD] + back[a, h, r, here]
                    target[a, here, h * HD : (h + 1) * HD] = total.astype(BF)

    rounds = (
        (y, lambda at: {"seq": z * 32 + x * 8 + at}),
        (z * 4 + x, lambda at: {"seq": at * 8 + y}),
        (sample, lambda at: {"dp": at}),
    )

    def gather(i, total):
        place, device = rounds[i]
        gathered[i, place] = total

        @pl.loop(1, 8)
        def _(step):
            remote(
                gathered.at[i, place],
                gathered.at[i, place],
                sum_send.at[i],
                sum_recv.at[i],
                device((place + step) % 8),
            ).start()

    def gathered_sum(i):
        wait_bytes(gathered.at[i, pl.ds(0, 7)], sum_recv.at[i])
        return jnp.sum(gathered[i], axis=0)

    own = jnp.sum(sums[...], axis=1)
    gather(0, jnp.concatenate([own, jnp.zeros_like(own)], axis=0))

    wait_bytes(got_head.at[pl.ds(0, 32)], head_recv)
    add_units(got_head, other, final_out)
    for g in range(2):
        for a in range(2):
            out_trade(a, g).start()

    gather(1, gathered_sum(0))
    wait_bytes(got_own, back_recv)
    add_units(got_own, half, final_own)
    for g in range(2):
        for a in range(2):
            out_own(a, g).start()

    gather(2, gathered_sum(1))
    wait_bytes(got_token.at[pl.ds(0, 32)], token_recv)

    for g in range(2):
        for a in range(2):
            out_trade(a, g).wait_recv()

    for block in range(4):
        moved = units_to_rows(got_token, block)
        here = pl.ds(block * 32, 32)
        for a in range(2):
            for h in range(8):
                columns = slice(h * HD, (h + 1) * HD)
                total = moved[h * 32 : h * 32 + 32, a * HD : (a + 1) * HD] + final_in[
                    a, here, columns
                ].astype(F32)
                final_sum[a, here, columns] = total.astype(BF)

    sum_copies = [
        pltpu.make_async_copy(
            final_sum.at[a], outputs[a].at[:, pl.ds(other * HALF, HALF)], sum_sem.at[a]
        )
        for a in range(2)
    ]
    for copy in sum_copies:
        copy.start()
    gain_grads[...] = gathered_sum(2)[0:4]

    for i in range(3):
        wait_bytes(gathered.at[i, pl.ds(0, 7)], sum_send.at[i])
    for g in range(2):
        out_trade(2, g).wait_recv()
        for a in range(3):
            trade_copy(a, g).wait_send()
            out_trade(a, g).wait_send()
            out_own(a, g).wait()
        wait_bytes(send_o.at[g, pl.ds(0, SEQ - 1)], o_send.at[g])
    wait_bytes(send_native.at[pl.ds(0, 47)], native_send)
    wait_bytes(send_relay.at[pl.ds(0, 31)], relay_send)
    wait_bytes(got_d.at[:, pl.ds(0, SEQ - 1)], d_send)
    wait_bytes(got_head.at[pl.ds(0, 31)], head_send)
    wait_bytes(got_token.at[pl.ds(0, 31)], token_send)
    wait_bytes(got_own.at[pl.ds(0, 63)], back_send)
    mixed_out.wait()
    for copy in sum_copies:
        copy.wait()


def write_out(*refs):
    sources, targets, sem = refs[:5], refs[5:10], refs[10]
    copies = [
        pltpu.make_async_copy(source, target, sem.at[i])
        for i, (source, target) in enumerate(zip(sources, targets))
    ]
    for copy in copies:
        copy.start()
    for copy in copies:
        copy.wait()


def body(query, key, value, gains, d_mixed):
    wide = (ROWS, WIDTH)
    hbm_spec = pl.BlockSpec(memory_space=pltpu.HBM)
    any_spec = pl.BlockSpec(memory_space=pl.ANY)
    vmem_spec = pl.BlockSpec(memory_space=pltpu.VMEM)
    dma = pltpu.SemaphoreType.DMA
    shapes = [jax.ShapeDtypeStruct(wide, BF)] * 4 + [jax.ShapeDtypeStruct((4, HD), F32)]
    results = pl.pallas_call(
        kernel,
        out_shape=shapes,
        in_specs=[hbm_spec] * 5,
        out_specs=[any_spec, any_spec, any_spec, any_spec, vmem_spec],
        scratch_shapes=[
            pltpu.VMEM((4, HD), F32),
            pltpu.VMEM((len(SELECTORS), 256, 256), BF),
            pltpu.VMEM((2, ROWS, WIDTH), BF),
            pltpu.VMEM((3, 2, ROWS, HALF), BF),
            pltpu.VMEM(wide, BF),
            pltpu.VMEM((8, 256, 256), F32),
            pltpu.VMEM((2, 4, 2, 4, 32, HD), BF),
            pltpu.VMEM((SEQ, 2, 2, 16, HD), BF),
            pltpu.VMEM((SEQ, 2, 16, HD), BF),
            pltpu.VMEM((2, SEQ, 16, HD), BF),
            pltpu.VMEM((FRAMES, 2, 2, 2, 16, HD), BF),
            pltpu.VMEM((4, FRAMES, 16, HD), BF),
            pltpu.VMEM((2, 2, 8, 4, 4, 8, HD), F32),
            pltpu.VMEM((4, 4, 2, 16, HD), BF),
            pltpu.VMEM((4, 4, 2, 16, HD), BF),
            pltpu.VMEM((2, 2, 8, 4, 4, 8, HD), F32),
            pltpu.VMEM(wide, BF),
            pltpu.VMEM((4, FRAMES, 16, HD), BF),
            pltpu.VMEM((2, FRAMES, 2, 2, 16, HD), BF),
            pltpu.VMEM((2, SEQ, 16, HD), BF),
            pltpu.VMEM((SEQ, 2, 16, HD), BF),
            pltpu.VMEM((SEQ, 2, 16, HD), BF),
            pltpu.VMEM((SEQ, 2, 16, HD), BF),
            pltpu.VMEM((4, 2, 4, 32, HD), BF),
            pltpu.VMEM((2, 8, 2, ROWS, HD), F32),
            pltpu.VMEM((3, ROWS, HALF), BF),
            pltpu.VMEM((3, ROWS, HALF), BF),
            pltpu.VMEM((2, ROWS, HALF), BF),
            pltpu.VMEM((2, ROWS, HALF), BF),
            pltpu.VMEM((4, 8, HD), F32),
            pltpu.VMEM((3, 8, 8, HD), F32),
            dma,
            dma((2,)),
            dma((3, 2)),
            dma((3, 2)),
            dma((3, 2)),
            dma,
            dma,
            dma,
            dma,
            dma,
            dma((2,)),
            dma((4,)),
            dma,
            dma((2,)),
            dma,
            dma,
            dma,
            dma,
            dma,
            dma,
            dma((3, 2)),
            dma((3, 2)),
            dma((3, 2)),
            dma((2,)),
            dma((3,)),
            dma((3,)),
        ],
        compiler_params=pltpu.CompilerParams(
            collective_id=0, has_side_effects=True, vmem_limit_bytes=103 * 2**19
        ),
        cost_estimate=pl.CostEstimate(flops=2 * 10**9, bytes_accessed=2**22, transcendentals=10**6),
        name="space_time_attention",
    )(query.reshape(wide), key.reshape(wide), value.reshape(wide), gains, d_mixed.reshape(wide))
    mixed, query_grad, key_grad, value_grad, gain_grads = pl.pallas_call(
        write_out,
        out_shape=shapes,
        in_specs=[vmem_spec] * 5,
        out_specs=[hbm_spec] * 5,
        scratch_shapes=[dma((5,))],
        compiler_params=pltpu.CompilerParams(vmem_limit_bytes=4 * 2**20),
        name="write_out",
    )(*results)
    return (
        mixed.reshape(d_mixed.shape),
        query_grad.reshape(query.shape),
        key_grad.reshape(key.shape),
        value_grad.reshape(value.shape),
        gain_grads,
    )


def solution(mesh):
    placed = (
        P("dp", "seq", None),
        P("dp", "seq", None),
        P("dp", "seq", None),
        P(),
        P("dp", None, "seq", None, None),
    )
    return jax.shard_map(
        body,
        mesh=mesh,
        in_specs=placed,
        out_specs=(
            P("dp", None, "seq", None, None),
            P("dp", "seq", None),
            P("dp", "seq", None),
            P("dp", "seq", None),
            P(),
        ),
        check_vma=False,
    )
```

time: 137 us -> 120 us (0.88)
  Pallas kernels: 127 us -> 118 us
  local copies, waits for them, and re-layouts: 8.59 us -> 0.67 us
    pallas_call x1 -> x2, Pallas kernels: 127 us -> 118 us  [the longest x1 117 us: body(): pl.pallas_call(kernel, out_shape=shapes, in_specs=[hbm_spec] * 5, out_spe...]
    unnamed x15 -> x2, local copies, waits for them, and re-layouts: 8.59 us -> 0.67 us
where the time goes in v1:
time: 120 us
  Pallas kernels  118 us (98%)
    pallas_call x1, Pallas kernels, body(): pl.pallas_call(kernel, out_shape=shapes, in_specs=[hbm_spec] * 5, out_spe...  117 us

profile of v1, /device:TPU:1, one launch (start us, length us, event | category | flops | bytes accessed | tf_op | source)
XLA Modules:
  0.0 119.7 jit_solution(16210573236273220210)
XLA Ops:
  0.6 0.0 copy-start
  0.6 0.7 copy-done
  1.3 117.1 %space_time_attention.1 = (bf16[128,2048]{1,0:T(8,128)(2,1)S(1)}, bf16[128,2048]{1,0:T(8,128)(2,1)S(1)}, bf16[128,2048]{1,0:T(8,128)(2,1)S(1)}, bf16[128,2048]{1,0:T(8,128)(2,1)S(1)}, f32[4,128]{1,0:T(4,128)S(1)}) custom-call(bf16[128,2048]{1,0:T(8,128)(2,1)} %bitcast.8, bf16[128,2048]{1,0:T(8,128)(2,1)} %bitcast.9, bf16[128,2048]{1,0:T(8,128)(2,1)} %bitcast.10, ...), custom_call_target="tpu_custom_call" | custom-call | flops 2000000000 | bytes 4194304 | tf_op jit(solution)/shard_map/space_time_attention/pallas_call | solution.py:589
  118.4 1.4 %write_out.1 = (bf16[128,2048]{1,0:T(8,128)(2,1)}, bf16[128,2048]{1,0:T(8,128)(2,1)}, bf16[128,2048]{1,0:T(8,128)(2,1)}, bf16[128,2048]{1,0:T(8,128)(2,1)}, f32[4,128]{1,0:T(4,128)}) custom-call(bf16[128,2048]{1,0:T(8,128)(2,1)S(1)} %get-tuple-element.15.refs_0_, bf16[128,2048]{1,0:T(8,128)(2,1)S(1)} %get-tuple-element.16.refs_1_, ...), custom_call_target="tpu_custom_call" | custom-call | tf_op jit(solution)/shard_map/write_out/pallas_call | solution.py:659
Async XLA Ops:
  0.6 0.7 copy-start

commit v2 on v1

--- a/solution.py
+++ b/solution.py
@@ -95,11 +95,11 @@
     query, key, value, gains_in, d_mixed,
     mixed, query_grad, key_grad, value_grad, gain_grads,
     gains, select, native, frame, d_time, probs, o_space, send_native, send_relay, send_o, got_qk, got_o,
-    time_qk, time_o, time_d, time_dqk, time_mixed, send_d, send_dqk, got_d, got_own, got_head,
-    got_token, d_space, back, final_out, final_own, final_in, final_sum, sums, gathered,
+    time_qk, time_o, time_d, time_dqk, time_mixed, send_d, send_dqk, got_d, got_own, got_cross,
+    d_space, back, final_out, final_own, final_in, final_sum, sums, gathered,
     gains_sem, native_sem, own_sem, trade_send, trade_recv, mixed_in_sem, mixed_sem,
     native_send, relay_send, qk_recv, o_send, o_recv, d_send, d_recv,
-    head_send, token_send, back_send, head_recv, token_recv, back_recv,
+    cross_send, back_send, cross_recv, back_recv,
     out_sem, out_send, out_recv, sum_sem, sum_send, sum_recv,
 ):
     me = lax.axis_index("seq")
@@ -174,8 +174,7 @@
             own_copy(a, g).start()
     mixed_in = pltpu.make_async_copy(d_mixed, d_time, mixed_in_sem)
     mixed_in.start()
-    got_head[...] = jnp.zeros_like(got_head)
-    got_token[...] = jnp.zeros_like(got_token)
+    got_cross[...] = jnp.zeros_like(got_cross)
 
     barrier = pltpu.get_barrier_semaphore()
 
@@ -228,21 +227,38 @@
         for block in range(4):
             rows_to_units(lambda a: native.at[a], block, hh * HALF, put)
 
+    pltpu.make_async_copy(send_native.at[me], got_qk.at[frame_at, half], qk_recv).start()
+
+    @pl.loop(1, 32)
+    def _(step):
+        to = near_peer(step)
+        remote(send_native.at[to], got_qk.at[frame_at, half], native_send, qk_recv, to).start()
+
     @pl.loop(0, 2)
     def _(g):
         for a in range(3):
             own_copy(a, g).wait()
             trade_copy(a, g).wait_recv()
 
-        @pl.when(g == 0)
+        @pl.when(g == 1)
         def _():
-            pltpu.make_async_copy(send_native.at[me], got_qk.at[frame_at, half], qk_recv).start()
+            def put_relay(devices, a, units):
+                send_relay[devices, a] = units
+
+            for block in range(4):
+                rows_to_units(lambda a: frame.at[a, other], block, 0, put_relay)
+
+            pltpu.make_async_copy(send_relay.at[me], got_qk.at[frame_at, other, half], qk_recv).start()
 
             @pl.loop(1, 32)
             def _(step):
                 to = near_peer(step)
-                remote(send_native.at[to], got_qk.at[frame_at, half], native_send, qk_recv, to).start()
-
+                remote(
+                    send_relay.at[to], got_qk.at[frame_at, other, half], relay_send, qk_recv, to
+                ).start()
+
+        @pl.when(g == 0)
+        def _():
             @pl.loop(0, 32)
             def _(step):
                 to = far_peer(step)
@@ -276,20 +292,31 @@
                 send_o.at[g, to], got_o.at[slot, frame_at], o_send.at[g], o_recv.at[slot], to
             ).start()
 
-    def put_relay(devices, a, units):
-        send_relay[devices, a] = units
-
-    for block in range(4):
-        rows_to_units(lambda a: frame.at[a, other], block, 0, put_relay)
-
-    pltpu.make_async_copy(send_relay.at[me], got_qk.at[frame_at, other, half], qk_recv).start()
-
-    @pl.loop(1, 32)
-    def _(step):
-        to = near_peer(step)
-        remote(
-            send_relay.at[to], got_qk.at[frame_at, other, half], relay_send, qk_recv, to
+    def send_cross(hh):
+        for part in range(4):
+            units = [time_dqk[hh, a, :, :, part].reshape(256, HD).astype(BF) for a in range(2)]
+            moved = dot(select[7], jnp.concatenate(units, axis=1), NN).astype(BF)
+            for a in range(2):
+                send_dqk[hh, pl.ds(part * 8, 8), :, a] = moved[:, a * HD : (a + 1) * HD].reshape(
+                    8, 2, 16, HD
+                )
+        own_kind = half if hh == 0 else 1 - half
+        pltpu.make_async_copy(
+            send_dqk.at[hh, frame_at, 1 - hh], got_cross.at[own_kind, me], cross_recv.at[own_kind]
         ).start()
+
+        @pl.loop(1, FRAMES)
+        def _(step):
+            to = frame_peer(step)
+            side = ((y + 11 - 2 * (to % 4)) % 8) // 4
+            kind = side if hh == 0 else 1 - side
+            remote(
+                send_dqk.at[hh, to, 1 - hh],
+                got_cross.at[kind, me],
+                cross_send,
+                cross_recv.at[kind],
+                to * 2 + side,
+            ).start()
 
     wait_bytes(got_qk, qk_recv)
     for hh in range(2):
@@ -370,44 +397,22 @@
 
         pl.loop(1, FRAMES)(send_one)
 
+        @pl.when(t == 2)
+        def _():
+            send_cross(0)
+
     mixed_out = pltpu.make_async_copy(time_mixed, mixed, mixed_sem)
     mixed_out.start()
 
-    for hh in range(2):
-        for part in range(4):
-            units = [time_dqk[hh, a, :, :, part].reshape(256, HD).astype(BF) for a in range(2)]
-            moved = dot(select[7], jnp.concatenate(units, axis=1), NN).astype(BF)
-            for a in range(2):
-                send_dqk[hh, pl.ds(part * 8, 8), :, a] = moved[:, a * HD : (a + 1) * HD].reshape(
-                    8, 2, 16, HD
-                )
-
-    def nearer(frame_to):
-        return ((y + 11 - 2 * (frame_to % 4)) % 8) // 4
-
-    pltpu.make_async_copy(send_dqk.at[half, frame_at, other], got_head.at[me], head_recv).start()
-
-    @pl.loop(1, FRAMES)
-    def _(step):
-        to = frame_peer(step)
-        side = nearer(to)
-        remote(
-            send_dqk.at[side, to, 1 - side], got_head.at[me], head_send, head_recv, to * 2 + side
-        ).start()
-
+    send_cross(1)
     pltpu.make_async_copy(send_dqk.at[half, frame_at, half], got_own.at[me], back_recv).start()
     remote(
         send_dqk.at[other, frame_at, other], got_own.at[me], back_send, back_recv, partner
     ).start()
-    pltpu.make_async_copy(send_dqk.at[other, frame_at, half], got_token.at[me], token_recv).start()
 
     @pl.loop(1, FRAMES)
     def _(step):
         to = frame_peer(step)
-        side = nearer(to)
-        remote(
-            send_dqk.at[1 - side, to, side], got_token.at[me], token_send, token_recv, to * 2 + side
-        ).start()
         for hh in range(2):
             remote(
                 send_dqk.at[hh, to, hh], got_own.at[me], back_send, back_recv, to * 2 + hh
@@ -506,45 +511,40 @@
     own = jnp.sum(sums[...], axis=1)
     gather(0, jnp.concatenate([own, jnp.zeros_like(own)], axis=0))
 
-    wait_bytes(got_head.at[pl.ds(0, 32)], head_recv)
-    add_units(got_head, other, final_out)
-    for g in range(2):
-        for a in range(2):
+    wait_bytes(got_cross.at[0, pl.ds(0, 32)], cross_recv.at[0])
+    add_units(got_cross.at[0], other, final_out)
+    gather(1, gathered_sum(0))
+    for a in range(2):
+        for g in range(2):
             out_trade(a, g).start()
 
-    gather(1, gathered_sum(0))
+    gather(2, gathered_sum(1))
     wait_bytes(got_own, back_recv)
     add_units(got_own, half, final_own)
     for g in range(2):
         for a in range(2):
             out_own(a, g).start()
 
-    gather(2, gathered_sum(1))
-    wait_bytes(got_token.at[pl.ds(0, 32)], token_recv)
-
-    for g in range(2):
-        for a in range(2):
+    wait_bytes(got_cross.at[1, pl.ds(0, 32)], cross_recv.at[1])
+
+    def sum_copy(a):
+        return pltpu.make_async_copy(
+            final_sum.at[a], outputs[a].at[:, pl.ds(other * HALF, HALF)], sum_sem.at[a]
+        )
+
+    added = [units_to_rows(got_cross.at[1], block) for block in range(4)]
+    for a in range(2):
+        for g in range(2):
             out_trade(a, g).wait_recv()
-
-    for block in range(4):
-        moved = units_to_rows(got_token, block)
-        here = pl.ds(block * 32, 32)
-        for a in range(2):
+        for block in range(4):
+            here = pl.ds(block * 32, 32)
             for h in range(8):
                 columns = slice(h * HD, (h + 1) * HD)
-                total = moved[h * 32 : h * 32 + 32, a * HD : (a + 1) * HD] + final_in[
+                total = added[block][h * 32 : h * 32 + 32, a * HD : (a + 1) * HD] + final_in[
                     a, here, columns
                 ].astype(F32)
                 final_sum[a, here, columns] = total.astype(BF)
-
-    sum_copies = [
-        pltpu.make_async_copy(
-            final_sum.at[a], outputs[a].at[:, pl.ds(other * HALF, HALF)], sum_sem.at[a]
-        )
-        for a in range(2)
-    ]
-    for copy in sum_copies:
-        copy.start()
+        sum_copy(a).start()
     gain_grads[...] = gathered_sum(2)[0:4]
 
     for i in range(3):
@@ -559,12 +559,11 @@
     wait_bytes(send_native.at[pl.ds(0, 47)], native_send)
     wait_bytes(send_relay.at[pl.ds(0, 31)], relay_send)
     wait_bytes(got_d.at[:, pl.ds(0, SEQ - 1)], d_send)
-    wait_bytes(got_head.at[pl.ds(0, 31)], head_send)
-    wait_bytes(got_token.at[pl.ds(0, 31)], token_send)
+    wait_bytes(got_cross.at[:, pl.ds(0, 31)], cross_send)
     wait_bytes(got_own.at[pl.ds(0, 63)], back_send)
     mixed_out.wait()
-    for copy in sum_copies:
-        copy.wait()
+    for a in range(2):
+        sum_copy(a).wait()
 
 
 def write_out(*refs):
@@ -613,8 +612,7 @@
             pltpu.VMEM((2, FRAMES, 2, 2, 16, HD), BF),
             pltpu.VMEM((2, SEQ, 16, HD), BF),
             pltpu.VMEM((SEQ, 2, 16, HD), BF),
-            pltpu.VMEM((SEQ, 2, 16, HD), BF),
-            pltpu.VMEM((SEQ, 2, 16, HD), BF),
+            pltpu.VMEM((2, SEQ, 2, 16, HD), BF),
             pltpu.VMEM((4, 2, 4, 32, HD), BF),
             pltpu.VMEM((2, 8, 2, ROWS, HD), F32),
             pltpu.VMEM((3, ROWS, HALF), BF),
@@ -639,9 +637,7 @@
             dma((2,)),
             dma,
             dma,
-            dma,
-            dma,
-            dma,
+            dma((2,)),
             dma,
             dma((3, 2)),
             dma((3, 2)),

time: 120 us -> 116 us (0.967)
  Pallas kernels: 118 us -> 114 us
    pallas_call x1, Pallas kernels: 117 us -> 112 us  [body(): pl.pallas_call(kernel, out_shape=shapes, in_specs=[hbm_spec] * 5, out_spe...]
where the time goes in v2:
time: 116 us; the launch traced here: 115 us
  Pallas kernels  114 us (98%)
    pallas_call x1, Pallas kernels, body(): pl.pallas_call(kernel, out_shape=shapes, in_specs=[hbm_spec] * 5, out_spe...  112 us

profile of v2, /device:TPU:1, one launch (start us, length us, event | category | flops | bytes accessed | tf_op | source)
XLA Modules:
  0.0 115.0 jit_solution(17113554521693822050)
XLA Ops:
  0.6 0.0 copy-start
  0.6 0.7 copy-done
  1.3 112.3 %space_time_attention.1 = (bf16[128,2048]{1,0:T(8,128)(2,1)S(1)}, bf16[128,2048]{1,0:T(8,128)(2,1)S(1)}, bf16[128,2048]{1,0:T(8,128)(2,1)S(1)}, bf16[128,2048]{1,0:T(8,128)(2,1)S(1)}, f32[4,128]{1,0:T(4,128)S(1)}) custom-call(bf16[128,2048]{1,0:T(8,128)(2,1)} %bitcast.8, bf16[128,2048]{1,0:T(8,128)(2,1)} %bitcast.9, bf16[128,2048]{1,0:T(8,128)(2,1)} %bitcast.10, ...), custom_call_target="tpu_custom_call" | custom-call | flops 2000000000 | bytes 4194304 | tf_op jit(solution)/shard_map/space_time_attention/pallas_call | solution.py:588
  113.7 1.4 %write_out.1 = (bf16[128,2048]{1,0:T(8,128)(2,1)}, bf16[128,2048]{1,0:T(8,128)(2,1)}, bf16[128,2048]{1,0:T(8,128)(2,1)}, bf16[128,2048]{1,0:T(8,128)(2,1)}, f32[4,128]{1,0:T(4,128)}) custom-call(bf16[128,2048]{1,0:T(8,128)(2,1)S(1)} %get-tuple-element.15.refs_0_, bf16[128,2048]{1,0:T(8,128)(2,1)S(1)} %get-tuple-element.16.refs_1_, ...), custom_call_target="tpu_custom_call" | custom-call | tf_op jit(solution)/shard_map/write_out/pallas_call | solution.py:655
Async XLA Ops:
  0.6 0.7 copy-start

commit v3 on v2

--- a/solution.py
+++ b/solution.py
@@ -96,11 +96,11 @@
     mixed, query_grad, key_grad, value_grad, gain_grads,
     gains, select, native, frame, d_time, probs, o_space, send_native, send_relay, send_o, got_qk, got_o,
     time_qk, time_o, time_d, time_dqk, time_mixed, send_d, send_dqk, got_d, got_own, got_cross,
-    d_space, back, final_out, final_own, final_in, final_sum, sums, gathered,
+    d_space, back, final_out, final_own, final_in, sums, gathered,
     gains_sem, native_sem, own_sem, trade_send, trade_recv, mixed_in_sem, mixed_sem,
     native_send, relay_send, qk_recv, o_send, o_recv, d_send, d_recv,
     cross_send, back_send, cross_recv, back_recv,
-    out_sem, out_send, out_recv, sum_sem, sum_send, sum_recv,
+    out_sem, out_send, out_recv, sum_send, sum_recv,
 ):
     me = lax.axis_index("seq")
     sample = lax.axis_index("dp")
@@ -109,26 +109,44 @@
     other = 1 - half
     partner = me + 1 - 2 * half
 
-    def device_at(step, dy):
-        return ((z + step // 16) % 2) * 32 + ((x + (step // 4) % 4) % 4) * 8 + (y + 8 + dy) % 8
-
-    def peer(step):
-        return (
-            ((z + step // 32) % 2) * 32 + ((x + (step // 8) % 4) % 4) * 8 + (y + step % 8) % 8
-        )
-
-    def near_peer(step):
-        return device_at(step, (step % 4) * (2 * half - 1))
-
-    def far_peer(step):
-        return device_at(step, (step % 4 + 1) * (1 - 2 * half))
-
-    def frame_peer(step):
-        return (
-            ((z + step // 16) % 2) * 16
-            + ((x + (step // 4) % 4) % 4) * 4
-            + (y // 2 + step % 4) % 4
-        )
+    def each_peer(one):
+        @pl.loop(1, 8)
+        def _(at):
+            base = ((z + (8 - at) // 4) % 2) * 32 + ((x + (8 - at) % 4) % 4) * 8
+            for dy in (4, 3, 5, 2, 6, 1, 7, 0):
+                one(base + (y + dy) % 8)
+
+        for dy in (4, 3, 5, 2, 6, 1, 7):
+            one(z * 32 + x * 8 + (y + dy) % 8)
+
+    def each_frame(one):
+        @pl.loop(1, 8)
+        def _(at):
+            base = ((z + (8 - at) // 4) % 2) * 16 + ((x + (8 - at) % 4) % 4) * 4
+            for dy in (2, 1, 3, 0):
+                one(base + (y // 2 + dy) % 4)
+
+        for dy in (2, 1, 3):
+            one(z * 16 + x * 4 + (y // 2 + dy) % 4)
+
+    away = 2 * half - 1
+
+    def each_near(one):
+        @pl.loop(1, 8)
+        def _(at):
+            base = ((z + (8 - at) // 4) % 2) * 32 + ((x + (8 - at) % 4) % 4) * 8
+            for dy in (3, 2, 1, 0):
+                one(base + (y + 8 + dy * away) % 8)
+
+        for dy in (3, 2, 1):
+            one(z * 32 + x * 8 + (y + 8 + dy * away) % 8)
+
+    def each_far(one):
+        @pl.loop(0, 8)
+        def _(at):
+            base = ((z + (7 - at) // 4) % 2) * 32 + ((x + (7 - at) % 4) % 4) * 8
+            for dy in (4, 3, 2, 1):
+                one(base + (y + 8 - dy * away) % 8)
 
     def remote(source, target, send_sem, recv_sem, to):
         return pltpu.make_async_remote_copy(
@@ -178,12 +196,6 @@
 
     barrier = pltpu.get_barrier_semaphore()
 
-    @pl.loop(1, SEQ)
-    def _(step):
-        pl.semaphore_signal(
-            barrier, inc=1, device_id={"seq": peer(step)}, device_id_type=pl.DeviceIdType.MESH
-        )
-
     @pl.loop(1, DP)
     def _(step):
         pl.semaphore_signal(
@@ -192,6 +204,12 @@
             device_id={"dp": (sample + step) % DP},
             device_id_type=pl.DeviceIdType.MESH,
         )
+
+    each_peer(
+        lambda to: pl.semaphore_signal(
+            barrier, inc=1, device_id={"seq": to}, device_id_type=pl.DeviceIdType.MESH
+        )
+    )
 
     pl.semaphore_wait(barrier, SEQ - 1 + DP - 1)
 
@@ -229,10 +247,11 @@
 
     pltpu.make_async_copy(send_native.at[me], got_qk.at[frame_at, half], qk_recv).start()
 
-    @pl.loop(1, 32)
-    def _(step):
-        to = near_peer(step)
-        remote(send_native.at[to], got_qk.at[frame_at, half], native_send, qk_recv, to).start()
+    each_near(
+        lambda to: remote(
+            send_native.at[to], got_qk.at[frame_at, half], native_send, qk_recv, to
+        ).start()
+    )
 
     @pl.loop(0, 2)
     def _(g):
@@ -250,21 +269,23 @@
 
             pltpu.make_async_copy(send_relay.at[me], got_qk.at[frame_at, other, half], qk_recv).start()
 
-            @pl.loop(1, 32)
-            def _(step):
-                to = near_peer(step)
-                remote(
+            each_near(
+                lambda to: remote(
                     send_relay.at[to], got_qk.at[frame_at, other, half], relay_send, qk_recv, to
                 ).start()
+            )
 
         @pl.when(g == 0)
         def _():
-            @pl.loop(0, 32)
-            def _(step):
-                to = far_peer(step)
-                remote(
-                    send_native.at[to, half], got_qk.at[frame_at, half, half], native_send, qk_recv, to
+            each_far(
+                lambda to: remote(
+                    send_native.at[to, half],
+                    got_qk.at[frame_at, half, half],
+                    native_send,
+                    qk_recv,
+                    to,
                 ).start()
+            )
 
         @pl.loop(0, 4)
         def _(h):
@@ -285,12 +306,11 @@
         slot = g * 2 + half
         pltpu.make_async_copy(send_o.at[g, me], got_o.at[slot, frame_at], o_recv.at[slot]).start()
 
-        @pl.loop(1, SEQ)
-        def _(step):
-            to = peer(step)
-            remote(
+        each_peer(
+            lambda to: remote(
                 send_o.at[g, to], got_o.at[slot, frame_at], o_send.at[g], o_recv.at[slot], to
             ).start()
+        )
 
     def send_cross(hh):
         for part in range(4):
@@ -305,9 +325,7 @@
             send_dqk.at[hh, frame_at, 1 - hh], got_cross.at[own_kind, me], cross_recv.at[own_kind]
         ).start()
 
-        @pl.loop(1, FRAMES)
-        def _(step):
-            to = frame_peer(step)
+        def send_one(to):
             side = ((y + 11 - 2 * (to % 4)) % 8) // 4
             kind = side if hh == 0 else 1 - side
             remote(
@@ -317,6 +335,8 @@
                 cross_recv.at[kind],
                 to * 2 + side,
             ).start()
+
+        each_frame(send_one)
 
     wait_bytes(got_qk, qk_recv)
     for hh in range(2):
@@ -383,8 +403,7 @@
             moved = dot(select[3], time_d[:, :, part].reshape(256, HD), NN).astype(BF)
             send_d[t, pl.ds(part * 16, 16)] = moved.reshape(16, 16, HD)
 
-        def send_one(step):
-            to = frame_peer(step)
+        def send_one(to):
             remote(send_d.at[t, to], got_d.at[g, me], d_send, d_recv.at[g], to * 2 + hh).start()
 
         @pl.when(hh == half)
@@ -393,9 +412,9 @@
 
         @pl.when(hh != half)
         def _():
-            send_one(0)
-
-        pl.loop(1, FRAMES)(send_one)
+            send_one(frame_at)
+
+        each_frame(send_one)
 
         @pl.when(t == 2)
         def _():
@@ -410,13 +429,13 @@
         send_dqk.at[other, frame_at, other], got_own.at[me], back_send, back_recv, partner
     ).start()
 
-    @pl.loop(1, FRAMES)
-    def _(step):
-        to = frame_peer(step)
+    def send_own(to):
         for hh in range(2):
             remote(
                 send_dqk.at[hh, to, hh], got_own.at[me], back_send, back_recv, to * 2 + hh
             ).start()
+
+    each_frame(send_own)
 
     def out_own(a, g):
         return pltpu.make_async_copy(
@@ -527,11 +546,6 @@
 
     wait_bytes(got_cross.at[1, pl.ds(0, 32)], cross_recv.at[1])
 
-    def sum_copy(a):
-        return pltpu.make_async_copy(
-            final_sum.at[a], outputs[a].at[:, pl.ds(other * HALF, HALF)], sum_sem.at[a]
-        )
-
     added = [units_to_rows(got_cross.at[1], block) for block in range(4)]
     for a in range(2):
         for g in range(2):
@@ -540,11 +554,11 @@
             here = pl.ds(block * 32, 32)
             for h in range(8):
                 columns = slice(h * HD, (h + 1) * HD)
+                place = pl.ds(pl.multiple_of(other * HALF + h * HD, HD), HD)
                 total = added[block][h * 32 : h * 32 + 32, a * HD : (a + 1) * HD] + final_in[
                     a, here, columns
                 ].astype(F32)
-                final_sum[a, here, columns] = total.astype(BF)
-        sum_copy(a).start()
+                outputs[a][here, place] = total.astype(BF)
     gain_grads[...] = gathered_sum(2)[0:4]
 
     for i in range(3):
@@ -562,8 +576,6 @@
     wait_bytes(got_cross.at[:, pl.ds(0, 31)], cross_send)
     wait_bytes(got_own.at[pl.ds(0, 63)], back_send)
     mixed_out.wait()
-    for a in range(2):
-        sum_copy(a).wait()
 
 
 def write_out(*refs):
@@ -589,7 +601,7 @@
         kernel,
         out_shape=shapes,
         in_specs=[hbm_spec] * 5,
-        out_specs=[any_spec, any_spec, any_spec, any_spec, vmem_spec],
+        out_specs=[vmem_spec] * 5,
         scratch_shapes=[
             pltpu.VMEM((4, HD), F32),
             pltpu.VMEM((len(SELECTORS), 256, 256), BF),
@@ -618,7 +630,6 @@
             pltpu.VMEM((3, ROWS, HALF), BF),
             pltpu.VMEM((3, ROWS, HALF), BF),
             pltpu.VMEM((2, ROWS, HALF), BF),
-            pltpu.VMEM((2, ROWS, HALF), BF),
             pltpu.VMEM((4, 8, HD), F32),
             pltpu.VMEM((3, 8, 8, HD), F32),
             dma,
@@ -642,7 +653,6 @@
             dma((3, 2)),
             dma((3, 2)),
             dma((3, 2)),
-            dma((2,)),
             dma((3,)),
             dma((3,)),
         ],

time: 116 us -> 112 us (0.966)
  Pallas kernels: 114 us -> 110 us
    pallas_call x1, Pallas kernels: 112 us -> 109 us  [body(): pl.pallas_call(kernel, out_shape=shapes, in_specs=[hbm_spec] * 5, out_spe...]
where the time goes in v3:
time: 112 us
  Pallas kernels  110 us (98%)
    pallas_call x1, Pallas kernels, body(): pl.pallas_call(kernel, out_shape=shapes, in_specs=[hbm_spec] * 5, out_spe...  109 us

profile of v3, /device:TPU:1, one launch (start us, length us, event | category | flops | bytes accessed | tf_op | source)
XLA Modules:
  0.0 111.7 jit_solution(7660292420438871737)
XLA Ops:
  0.6 0.0 copy-start
  0.6 0.7 copy-done
  1.3 109.0 %space_time_attention.1 = (bf16[128,2048]{1,0:T(8,128)(2,1)S(1)}, bf16[128,2048]{1,0:T(8,128)(2,1)S(1)}, bf16[128,2048]{1,0:T(8,128)(2,1)S(1)}, bf16[128,2048]{1,0:T(8,128)(2,1)S(1)}, f32[4,128]{1,0:T(4,128)S(1)}) custom-call(bf16[128,2048]{1,0:T(8,128)(2,1)} %bitcast.8, bf16[128,2048]{1,0:T(8,128)(2,1)} %bitcast.9, bf16[128,2048]{1,0:T(8,128)(2,1)} %bitcast.10, ...), custom_call_target="tpu_custom_call" | custom-call | flops 2000000000 | bytes 4194304 | tf_op jit(solution)/shard_map/space_time_attention/pallas_call | solution.py:600
  110.4 1.4 %write_out.1 = (bf16[128,2048]{1,0:T(8,128)(2,1)}, bf16[128,2048]{1,0:T(8,128)(2,1)}, bf16[128,2048]{1,0:T(8,128)(2,1)}, bf16[128,2048]{1,0:T(8,128)(2,1)}, f32[4,128]{1,0:T(4,128)}) custom-call(bf16[128,2048]{1,0:T(8,128)(2,1)S(1)} %get-tuple-element.15.refs_0_, bf16[128,2048]{1,0:T(8,128)(2,1)S(1)} %get-tuple-element.16.refs_1_, ...), custom_call_target="tpu_custom_call" | custom-call | tf_op jit(solution)/shard_map/write_out/pallas_call | solution.py:665
Async XLA Ops:
  0.6 0.7 copy-start

commit v4 on v3

--- a/solution.py
+++ b/solution.py
@@ -253,6 +253,12 @@
         ).start()
     )
 
+    def two_at_once(one_head):
+        @pl.loop(0, 2)
+        def _(pair):
+            one_head(pair * 2)
+            one_head(pair * 2 + 1)
+
     @pl.loop(0, 2)
     def _(g):
         for a in range(3):
@@ -287,7 +293,7 @@
                 ).start()
             )
 
-        @pl.loop(0, 4)
+        @two_at_once
         def _(h):
             columns = pl.ds(pl.multiple_of(g * PART + h * HD, HD), HD)
             q_hat, _ = hat(frame[0, :, :, columns].reshape(256, HD).astype(F32))
@@ -468,7 +474,7 @@
             moved = dot(select[1], got_d[g, pl.ds(b * 16, 16)].reshape(256, HD), NN).astype(BF)
             d_space[:, :, b] = moved.reshape(4, 2, 32, HD)
 
-        @pl.loop(0, 4)
+        @two_at_once
         def _(h):
             columns = pl.ds(pl.multiple_of(g * PART + h * HD, HD), HD)
             q_hat, q_factor = hat(frame[0, :, :, columns].reshape(256, HD).astype(F32))

time: 112 us -> 112 us (level)
  no operation moved by 1% of the time
where the time goes in v4:
time: 112 us; the launch traced here: 111 us
  Pallas kernels  110 us (98%)
    pallas_call x1, Pallas kernels, body(): pl.pallas_call(kernel, out_shape=shapes, in_specs=[hbm_spec] * 5, out_spe...  109 us

profile of v4, /device:TPU:1, one launch (start us, length us, event | category | flops | bytes accessed | tf_op | source)
XLA Modules:
  0.0 111.3 jit_solution(14428612376533687712)
XLA Ops:
  0.6 0.0 copy-start
  0.6 0.7 copy-done
  1.3 108.7 %space_time_attention.1 = (bf16[128,2048]{1,0:T(8,128)(2,1)S(1)}, bf16[128,2048]{1,0:T(8,128)(2,1)S(1)}, bf16[128,2048]{1,0:T(8,128)(2,1)S(1)}, bf16[128,2048]{1,0:T(8,128)(2,1)S(1)}, f32[4,128]{1,0:T(4,128)S(1)}) custom-call(bf16[128,2048]{1,0:T(8,128)(2,1)} %bitcast.8, bf16[128,2048]{1,0:T(8,128)(2,1)} %bitcast.9, bf16[128,2048]{1,0:T(8,128)(2,1)} %bitcast.10, ...), custom_call_target="tpu_custom_call" | custom-call | flops 2000000000 | bytes 4194304 | tf_op jit(solution)/shard_map/space_time_attention/pallas_call | solution.py:606
  110.0 1.4 %write_out.1 = (bf16[128,2048]{1,0:T(8,128)(2,1)}, bf16[128,2048]{1,0:T(8,128)(2,1)}, bf16[128,2048]{1,0:T(8,128)(2,1)}, bf16[128,2048]{1,0:T(8,128)(2,1)}, f32[4,128]{1,0:T(4,128)}) custom-call(bf16[128,2048]{1,0:T(8,128)(2,1)S(1)} %get-tuple-element.15.refs_0_, bf16[128,2048]{1,0:T(8,128)(2,1)S(1)} %get-tuple-element.16.refs_1_, ...), custom_call_target="tpu_custom_call" | custom-call | tf_op jit(solution)/shard_map/write_out/pallas_call | solution.py:671
Async XLA Ops:
  0.6 0.7 copy-start
